TPU v7x, 768 devices: a whole 4x8x12 slice. The times are simulated.
768 devices in a mesh: wide: 32 (over x, y_hi, core), cell: 24 (over z, y_lo).
Axes of the slice: x: 4, y: 8 (y_hi: 4, y_lo: 2; y = y_hi * 2 + y_lo), z: 12, core: 2. Of those that a mesh axis runs over, the one named last changes fastest.
Arguments:
- green_pair: float32 [2, 2, 128, 24, 128, 128], P(None, None, 'wide', 'cell'), may hold values from -5 to 5
- coulomb: float32 [24, 2, 128, 128], P('cell'), may hold values from -0.5 to 0.5
- green_retarded: float32 [2, 128, 24, 2, 128, 128], P(None, 'wide', 'cell'), may hold values from -0.375 to 0.375
- offsets: int32 [24, 2], P('cell'), may hold values from -1 to 1, as said below
Outputs:
- dressed: float32 [2, 128, 24, 128, 128], P(None, 'wide', 'cell')
Inputs may be any that keep to these rules, and one draw needn't show every extreme that they name: Block row r stores its blocks at block columns r + offsets[r, 0] and r + offsets[r, 1], two different entries of -1, 0, 1 in increasing order. Every block row r with r even has offsets -1 and 1.
All inputs are finite; a program needn't handle non-finite values.
Results may differ from a plain program's by a relative error of at most 0.00014.
Values sent between devices are 32-bit elements; how exact they have to be, the bound alone decides.
A program may use at most 32 MiB of HBM per device.

v0:
```python
import functools
import math

import jax
import jax.numpy as jnp
import numpy as np
from jax import lax
from jax.experimental import pallas as pl
from jax.experimental.pallas import tpu as pltpu
from jax.sharding import PartitionSpec as P

F32 = jnp.float32
BF16 = jnp.bfloat16
MESH = pl.DeviceIdType.MESH
WIDE_PARTS = (4, 4, 2)
LOCAL = 4


def split(value):
    high = value.astype(BF16)
    return high, (value - high.astype(F32)).astype(BF16)


def dot3(first, second, transposed=False):
    dims = (((1,), (1 if transposed else 0,)), ((), ()))
    multiply = functools.partial(lax.dot_general, dimension_numbers=dims, preferred_element_type=F32)
    return multiply(first[0], second[0]) + (multiply(first[0], second[1]) + multiply(first[1], second[0]))


def tables(energies, tile):
    period = 2 * energies
    angle = np.outer(np.arange(period), np.arange(energies)) % period * (2.0 * math.pi / period)
    cos, sin = np.cos(angle), np.sin(angle)
    real = np.concatenate([cos, sin], axis=1).reshape(period // tile, tile, period)
    imag = np.concatenate([-sin, cos], axis=1).reshape(period // tile, tile, period)
    forward = np.concatenate([real, imag], axis=1)
    scale = 1.0 / (period * energies)
    inverse = scale * np.stack([np.concatenate([cos.T, -sin.T], axis=1), np.concatenate([sin.T, cos.T], axis=1)])
    result = []
    for table in (forward, inverse):
        table = table.astype(np.float32)
        high = table.astype(BF16)
        result += [high, (table - high.astype(np.float32)).astype(BF16)]
    return result


def kernel(
    green, coulomb, offsets, retarded, fwd_hi, fwd_lo, inv_hi, inv_lo, out,
    pack, pairs, lhat, psend, precv, below, above, vboth, vhi, vlo, sel, yy, zsend, srecv, qsend, sig, sigh, sigc,
    local_sem, small_send, small_recv, send_sem, a_sem, p_sem, up_sem, down_sem, s_sem, q_sem, h_sem, c_sem, fwd_sem,
):
    wide, cell = lax.axis_index("wide"), lax.axis_index("cell")
    cells = lax.axis_size("cell")
    nx, nh, nc = WIDE_PARTS
    ny = 2 * nh
    group = nx * nc
    plane = ny * group
    energies = green.shape[2] * nx * nh * nc
    times = 2 * energies
    order = green.shape[-1]
    core, yh, x = wide % nc, wide // nc % nh, wide // (nc * nh)
    yl, z = cell % 2, cell // 2
    y = 2 * yh + yl
    place = (y * nx + x) * nc + core
    up = (wide, (cell + 2) % cells)
    down = (wide, (cell + cells - 2) % cells)
    partner = (wide, cell + 1 - 2 * yl)

    def rows8(index):
        return pl.ds(pl.multiple_of(8 * index, 8), 8)

    def rise(g):
        return jnp.where(g % 2 == 1, (g + 1) // 2, (ny - g // 2) % ny)

    def peer(k):
        g, h = k // group, k % group
        y2, x2, c2 = (y + rise(g)) % ny, (x + h // nc) % nx, (core + h % nc) % nc
        return g, (x2 * nh + y2 // 2) * nc + c2, y2 % 2, (y2 * nx + x2) * nc + c2

    def remote(src, dst, send, recv, device):
        return pltpu.make_async_remote_copy(
            src_ref=src, dst_ref=dst, send_sem=send, recv_sem=recv, device_id=device, device_id_type=MESH
        )

    def await_bytes(like, sem):
        pltpu.make_async_copy(like, like, sem).wait()

    def chunk(g):
        y0 = (y + ny - rise(g)) % ny
        return pl.ds(pl.multiple_of(y0 * (8 * group), 8 * group), 8 * group)

    barrier = pltpu.get_barrier_semaphore()

    def greet(k, carry):
        g, wide2, yl2, place2 = peer(k)
        pl.semaphore_signal(barrier, inc=1, device_id=(wide2, 2 * z + yl2), device_id_type=MESH)
        return carry

    lax.fori_loop(1, plane, greet, 0)
    for device in (up, down):
        pl.semaphore_signal(barrier, inc=1, device_id=device, device_id_type=MESH)

    for pair in range(2):
        for part in range(2):
            for e in range(LOCAL):
                for i in range(2):
                    pack[pair, part, pl.ds(2 * e + i, plane, stride=8), :] = green[
                        pair, part, e, i * plane : (i + 1) * plane, :
                    ]
    for slot in range(2):
        sel[yl, slot] = jnp.where(jnp.full((8, order), offsets[0, slot], jnp.int32) != 0, 1.0, 0.0)
    vboth[yl] = coulomb[...]
    pl.semaphore_wait(barrier, plane + 1)

    def send_pairs(k, carry):
        g, wide2, yl2, place2 = peer(k)
        remote(
            pack.at[:, :, rows8(place2), :], pairs.at[:, :, yl, rows8(wide), :],
            send_sem.at[0], a_sem, (wide2, 2 * z + yl2),
        ).start()
        return carry

    lax.fori_loop(1, plane, send_pairs, 0)
    own = pltpu.make_async_copy(pack.at[:, :, rows8(place), :], pairs.at[:, :, yl, rows8(wide), :], local_sem.at[0])
    own.start()
    coulomb_copy = remote(vboth.at[yl], vboth.at[yl], small_send.at[0], small_recv.at[0], partner)
    coulomb_copy.start()
    masks_copy = remote(sel.at[yl], sel.at[yl], small_send.at[1], small_recv.at[1], partner)
    masks_copy.start()

    @pl.when(yl == 0)
    def _():
        sigc[...] = jnp.zeros_like(sigc)

    own.wait()
    await_bytes(pack.at[:, :, pl.ds(0, 8 * plane - 8), :], a_sem)

    tiles, tile = fwd_hi.shape[0], fwd_hi.shape[1] // 2

    def transform(r, carry):
        for i in range(2):
            lr, li, ur, ui = (pairs[a, b, r, pl.ds(i, energies, stride=2), :] for a in range(2) for b in range(2))
            rhs = split(jnp.concatenate([jnp.concatenate([lr, ur], 1), jnp.concatenate([li, -ui], 1)], 0))
            for m in range(tiles):
                both = dot3((fwd_hi[m], fwd_lo[m]), rhs)
                ar, ai = both[:tile, :order], both[tile:, :order]
                br, bi = both[:tile, order:], both[tile:, order:]
                rows = pl.ds(2 * m * tile + i, tile, stride=2)
                lhat[0, r, rows, :] = ar
                lhat[1, r, rows, :] = ai
                psend[0, r, rows, :] = ar * br + ai * bi
                psend[1, r, rows, :] = ai * br - ar * bi
        return carry

    lax.fori_loop(0, 2, transform, 0)

    def send_polar(k, carry):
        g, wide2, yl2, place2 = peer(k)
        remote(
            psend.at[:, :, rows8(place2), :], precv.at[:, :, rows8(place), :],
            send_sem.at[1], p_sem.at[g], (wide2, 2 * z + yl2),
        ).start()
        return carry

    pltpu.make_async_copy(psend.at[:, :, rows8(place), :], precv.at[:, :, rows8(place), :], p_sem.at[0]).start()
    lax.fori_loop(1, plane, send_polar, 0)

    coulomb_copy.wait()
    masks_copy.wait()
    for r in range(2):
        for slot in range(2):
            high, low = split(vboth[r, slot])
            vhi[r, :, slot * order : (slot + 1) * order] = high
            vlo[r, :, slot * order : (slot + 1) * order] = low

    def forward(g, carry):
        rows = chunk(g)
        await_bytes(precv.at[:, :, rows, :], p_sem.at[g])
        remote(precv.at[:, 1, rows, :], below.at[:, rows, :], fwd_sem.at[0], up_sem.at[g], up).start()
        remote(precv.at[:, 0, rows, :], above.at[:, rows, :], fwd_sem.at[1], down_sem.at[g], down).start()
        return carry

    lax.fori_loop(0, ny, forward, 0)
    has_below = jnp.where(z > 0, 1.0, 0.0).astype(F32)
    has_above = jnp.where(z < cells // 2 - 1, 1.0, 0.0).astype(F32)

    def from_right(g, carry):
        rows = chunk(g)
        await_bytes(below.at[:, rows, :], up_sem.at[g])
        await_bytes(above.at[:, rows, :], down_sem.at[g])

        def stacked(ref, *lead):
            return jnp.concatenate([ref[(part, *lead, rows, slice(None))] for part in range(2)], 0)

        lower, even, odd, upper = (
            stacked(below) * has_below, stacked(precv, 0), stacked(precv, 1), stacked(above) * has_above
        )
        first = jnp.where(sel[1, 0, 0:1, :] > 0.5, even, odd)
        second = jnp.where(sel[1, 1, 0:1, :] > 0.5, upper, odd)
        for r, slot, value in ((0, 0, lower), (0, 1, odd), (1, 0, first), (1, 1, second)):
            block = slice(slot * order, (slot + 1) * order)
            done = dot3(split(value), (vhi[r, :, block], vlo[r, :, block]), True)
            half = done.shape[0] // 2
            yy[r, slot, 0, rows, :] = done[:half]
            yy[r, slot, 1, rows, :] = done[half:]
        return carry

    lax.fori_loop(0, ny, from_right, 0)

    def from_left(r, carry):
        for t in range(LOCAL):
            columns = []
            for part in range(2):
                columns.append(jnp.concatenate(
                    [yy[r, slot, part, pl.ds(2 * t + i, plane, stride=8), :] for slot in range(2) for i in range(2)], 0
                ))
            done = dot3((vhi[r], vlo[r]), split(jnp.concatenate(columns, 1)))
            for part in range(2):
                for i in range(2):
                    zsend[part, r, pl.ds(2 * t + i, plane, stride=8), :] = done[
                        i * plane : (i + 1) * plane, part * order : (part + 1) * order
                    ]
        return carry

    lax.fori_loop(0, 2, from_left, 0)

    def send_screened(k, carry):
        g, wide2, yl2, place2 = peer(k)
        remote(
            zsend.at[:, :, rows8(place2), :], srecv.at[:, :, rows8(place), :],
            send_sem.at[2], s_sem, (wide2, 2 * z + yl2),
        ).start()
        return carry

    lax.fori_loop(1, plane, send_screened, 0)
    own = pltpu.make_async_copy(zsend.at[:, :, rows8(place), :], srecv.at[:, :, rows8(place), :], local_sem.at[1])
    own.start()
    own.wait()
    await_bytes(zsend.at[:, :, pl.ds(0, 8 * plane - 8), :], s_sem)

    def back(r, carry):
        columns = []
        for i in range(2):
            rows = pl.ds(i, times, stride=2)
            lr, li, sr, si = lhat[0, r, rows, :], lhat[1, r, rows, :], srecv[0, r, rows, :], srecv[1, r, rows, :]
            columns.append(jnp.concatenate([lr * sr - li * si, lr * si + li * sr], 0))
        rhs = split(jnp.concatenate(columns, 1))
        for part in range(2):
            done = dot3((inv_hi[part], inv_lo[part]), rhs)
            for i in range(2):
                qsend[part, r, pl.ds(i, energies, stride=2), :] = done[:, i * order : (i + 1) * order]
        return carry

    lax.fori_loop(0, 2, back, 0)

    def send_sigma(k, carry):
        g, wide2, yl2, place2 = peer(k)
        remote(
            qsend.at[:, 1 - yl2, rows8(wide2), :], sig.at[:, rows8(place), :],
            send_sem.at[3], q_sem.at[g], (wide2, 2 * z + yl2),
        ).start()
        return carry

    pltpu.make_async_copy(qsend.at[:, 1 - yl, rows8(wide), :], sig.at[:, rows8(place), :], q_sem.at[0]).start()
    lax.fori_loop(1, plane, send_sigma, 0)

    along = (wide, (cell + cells + 2 - 4 * yl) % cells)

    def spread(g, carry):
        rows = chunk(g)
        await_bytes(sig.at[:, rows, :], q_sem.at[g])
        remote(sig.at[:, rows, :], sigh.at[:, rows, :], fwd_sem.at[2], h_sem.at[g], along).start()

        @pl.when(yl == 0)
        def _():
            remote(sig.at[:, rows, :], sigc.at[:, rows, :], fwd_sem.at[3], c_sem.at[g], partner).start()

        return carry

    lax.fori_loop(0, ny, spread, 0)

    @pl.when(yl == 1)
    def _():
        def arrive(g, carry):
            await_bytes(sigc.at[:, chunk(g), :], c_sem.at[g])
            return carry

        lax.fori_loop(0, ny, arrive, 0)

    even = yl == 0

    def term(e, slot, sr, si):
        gr, gi = retarded[0, e, slot], retarded[1, e, slot]
        left = dot3(
            split(jnp.concatenate([gr, gi], 1)),
            split(jnp.concatenate([jnp.concatenate([sr, si], 1), jnp.concatenate([-si, sr], 1)], 0)),
        )
        return dot3(
            split(left),
            split(jnp.concatenate([jnp.concatenate([gr, -gi], 1), jnp.concatenate([gi, gr], 1)], 0)),
            True,
        )

    def block(ref, e, part):
        return jnp.concatenate([ref[part, pl.ds(2 * e + i, plane, stride=8), :] for i in range(2)], 0)

    take_near = jnp.logical_or(jnp.full((8, order), yl, jnp.int32) == 0, sel[yl, 0] > 0.5)[0:1]
    take_far = jnp.logical_or(jnp.full((8, order), yl, jnp.int32) == 0, sel[yl, 1] > 0.5)[0:1]
    for e in range(LOCAL):
        sr, si = (jnp.where(take_near, block(sig, e, part), block(sigc, e, part)) for part in range(2))
        done = term(e, 1 - yl, sr, si)
        out[0, e] = done[:, :order]
        out[1, e] = done[:, order:]

    def arrive_far(g, carry):
        await_bytes(sigh.at[:, chunk(g), :], h_sem.at[g])
        return carry

    lax.fori_loop(0, ny, arrive_far, 0)
    has_far = jnp.where(even, has_below, has_above)
    for e in range(LOCAL):
        sr, si = (
            jnp.where(take_far, block(sigh, e, part) * has_far, block(sigc, e, part)) for part in range(2)
        )
        done = term(e, yl, sr, si)
        out[0, e] += done[:, :order]
        out[1, e] += done[:, order:]

    await_bytes(pack.at[:, :, pl.ds(0, 8 * plane - 8), :], send_sem.at[0])
    await_bytes(psend.at[:, :, pl.ds(0, 8 * plane - 8), :], send_sem.at[1])
    await_bytes(zsend.at[:, :, pl.ds(0, 8 * plane - 8), :], send_sem.at[2])
    await_bytes(sig.at[:, pl.ds(0, 8 * plane - 8), :], send_sem.at[3])
    await_bytes(below, fwd_sem.at[0])
    await_bytes(above, fwd_sem.at[1])
    await_bytes(sig, fwd_sem.at[2])

    @pl.when(yl == 0)
    def _():
        await_bytes(sig, fwd_sem.at[3])


def body(green_pair, coulomb, green_retarded, offsets):
    nx, nh, nc = WIDE_PARTS
    ny, plane = 2 * nh, 2 * nx * nh * nc
    order, local = green_pair.shape[-1], green_pair.shape[2]
    energies = local * nx * nh * nc
    tile = min(64, 2 * energies)
    full = 8 * plane
    consts = [jnp.asarray(value) for value in tables(energies, tile)]
    vmem = pl.BlockSpec(memory_space=pltpu.VMEM)
    smem = pl.BlockSpec(memory_space=pltpu.SMEM)
    dma = pltpu.SemaphoreType.DMA
    dressed = pl.pallas_call(
        kernel,
        out_shape=jax.ShapeDtypeStruct((2, local, order, order), F32),
        in_specs=[vmem, vmem, smem, vmem, vmem, vmem, vmem, vmem],
        out_specs=vmem,
        scratch_shapes=[
            pltpu.VMEM((2, 2, full, order), F32),
            pltpu.VMEM((2, 2, 2, full // 2, order), F32),
            pltpu.VMEM((2, 2, full, order), F32),
            pltpu.VMEM((2, 2, full, order), F32),
            pltpu.VMEM((2, 2, full, order), F32),
            pltpu.VMEM((2, full, order), F32),
            pltpu.VMEM((2, full, order), F32),
            pltpu.VMEM((2, 2, order, order), F32),
            pltpu.VMEM((2, order, 2 * order), BF16),
            pltpu.VMEM((2, order, 2 * order), BF16),
            pltpu.VMEM((2, 2, 8, order), F32),
            pltpu.VMEM((2, 2, 2, full, order), F32),
            pltpu.VMEM((2, 2, full, order), F32),
            pltpu.VMEM((2, 2, full, order), F32),
            pltpu.VMEM((2, 2, full // 2, order), F32),
            pltpu.VMEM((2, full, order), F32),
            pltpu.VMEM((2, full, order), F32),
            pltpu.VMEM((2, full, order), F32),
            dma((2,)), dma((2,)), dma((2,)), dma((4,)), dma, dma((ny,)), dma((ny,)), dma((ny,)),
            dma, dma((ny,)), dma((ny,)), dma((ny,)), dma((4,)),
        ],
        compiler_params=pltpu.CompilerParams(
            collective_id=0, has_side_effects=True, vmem_limit_bytes=40 * 1024 * 1024
        ),
    )(green_pair[:, :, :, 0], coulomb[0], offsets, green_retarded[:, :, 0], *consts)
    return dressed[:, :, None]


def solution(mesh):
    placed = (
        P(None, None, "wide", "cell", None, None),
        P("cell", None, None, None),
        P(None, "wide", "cell", None, None, None),
        P("cell", None),
    )
    return jax.shard_map(
        body,
        mesh=mesh,
        in_specs=placed,
        out_specs=P(None, "wide", "cell", None, None),
        check_vma=False,
    )
```

profile of v0, /device:TPU:56, one launch (start us, length us, event | category | flops | bytes accessed | tf_op | source)
XLA Modules:
  0.0 145.4 jit_solution(16100629232726694054)
XLA Ops:
  0.0 0.0 copy-start.7
  0.0 0.7 copy-done.7
  0.7 0.0 copy-start
  0.7 1.2 copy-done
  1.9 0.0 copy-start.1
  1.9 1.2 copy-done.1
  3.1 0.0 copy-start.2
  3.1 0.9 copy-done.2
  4.1 0.0 copy-start.3
  4.1 0.9 copy-done.3
  5.0 0.0 copy-start.4
  5.0 0.9 copy-done.4
  6.0 0.0 copy-start.5
  6.0 0.9 copy-done.5
  6.9 0.0 copy-start.6
  6.9 0.9 copy-done.6
  7.8 136.8 %shard_map.82 = f32[2,4,128,128]{3,2,1,0:T(8,128)S(1)} custom-call(f32[2,2,4,128,128]{4,3,2,1,0:T(8,128)S(1)} %bitcast.7, f32[2,128,128]{2,1,0:T(8,128)S(1)} %bitcast.9, s32[1,2]{1,0:T(1,128)S(1)} %copy-done.7, f32[2,4,2,128,128]{4,3,2,1,0:T(8,128)S(1)} %bitcast.8, bf16[4,128,256]{2,1,0:T(8,128)(2,1)S(1)} %copy-done.5, bf16[4,128,256]{2,1,0:T(8,128)(2,1)S(1)} %copy-done.4, ...), custom_call_target="tpu_custom_call" | custom-call | tf_op jit(solution)/shard_map/pallas_call | solution.py:353
  144.6 0.8 copy.11
Async XLA Ops:
  0.0 0.7 copy-start.7
  0.7 1.2 copy-start
  1.9 1.2 copy-start.1
  3.1 0.9 copy-start.2
  4.1 0.9 copy-start.3
  5.0 0.9 copy-start.4
  6.0 0.9 copy-start.5
  6.9 0.9 copy-start.6
where the time goes:
time: 147 us; the launch traced here: 145 us
  Pallas kernels  137 us (93%)
  local copies, waits for them, and re-layouts  8.6 us (6%)
    pallas_call x1, Pallas kernels, body(): pl.pallas_call(kernel, out_shape=jax.ShapeDtypeStruct((2, local, order, o...  137 us
    unnamed x17, local copies, waits for them, and re-layouts  8.6 us

commit v1 on v0

v1 whole, which is shorter than its diff:
```python
import functools
import math

import jax
import jax.numpy as jnp
import numpy as np
from jax import lax
from jax.experimental import pallas as pl
from jax.experimental.pallas import tpu as pltpu
from jax.sharding import PartitionSpec as P

F32 = jnp.float32
BF16 = jnp.bfloat16
MESH = pl.DeviceIdType.MESH
WIDE_PARTS = (4, 4, 2)
LOCAL = 4


def split(value):
    high = value.astype(BF16)
    return high, (value - high.astype(F32)).astype(BF16)


def dot3(first, second, transposed=False):
    dims = (((1,), (1 if transposed else 0,)), ((), ()))
    multiply = functools.partial(lax.dot_general, dimension_numbers=dims, preferred_element_type=F32)
    return multiply(first[0], second[0]) + (multiply(first[0], second[1]) + multiply(first[1], second[0]))


def swap(value):
    tiles = value.reshape(value.shape[0] // 8, 8, value.shape[1])
    return jnp.concatenate([tiles[:, 4:], tiles[:, :4]], 1).reshape(value.shape)


def real_rows(shape):
    return lax.broadcasted_iota(jnp.int32, shape, 0) % 8 < 4


def tables(energies):
    period = 2 * energies
    angle = np.outer(np.arange(period), np.arange(energies)) % period * (2.0 * math.pi / period)

    def ordered(real_real, real_imag, imag_real, imag_imag):
        grid = np.array([[real_real, real_imag], [imag_real, imag_imag]])
        rows, columns = real_real.shape
        grid = grid.reshape(2, 2, rows // 4, 4, columns // 4, 4).transpose(2, 0, 3, 4, 1, 5)
        return grid.reshape(2 * rows, 2 * columns)

    cos, sin = np.cos(angle), np.sin(angle)
    scale = 1.0 / (period * energies)
    result = []
    for table in (ordered(cos, sin, -sin, cos), scale * ordered(cos.T, -sin.T, sin.T, cos.T)):
        table = table.astype(np.float32)
        high = table.astype(BF16)
        result += [high, (table - high.astype(np.float32)).astype(BF16)]
    return result


def kernel(
    green_in, coulomb_in, offsets_in, retarded_in, fwd_hi_in, fwd_lo_in, inv_hi_in, inv_lo_in, out,
    green, retarded, fwd_hi, fwd_lo, inv_hi, inv_lo, offsets,
    pack, pairs, lhat, psend, precv, below, above, vboth, vhi, vlo, sel, yy, zsend, srecv, qsend, sig, sigh,
    left_hi, left_lo, right_hi, right_lo,
    load_sem, local_sem, small_send, small_recv, send_sem, a_sem, p_sem, up_sem, down_sem, s_sem, q_sem, h_sem, fwd_sem,
):
    wide, cell = lax.axis_index("wide"), lax.axis_index("cell")
    cells = lax.axis_size("cell")
    nx, nh, nc = WIDE_PARTS
    ny = 2 * nh
    group = nx * nc
    plane = ny * group
    order = green.shape[-1]
    core, yh, x = wide % nc, wide // nc % nh, wide // (nc * nh)
    yl, z = cell % 2, cell // 2
    y = 2 * yh + yl
    place = (y * nx + x) * nc + core
    up, down = (wide, (cell + 2) % cells), (wide, (cell + cells - 2) % cells)
    has_up, has_down = z < cells // 2 - 1, z > 0
    partner = (wide, cell + 1 - 2 * yl)

    def rows8(index):
        return pl.ds(pl.multiple_of(8 * index, 8), 8)

    def rise(g):
        k = ny - 1 - g
        return jnp.where(k % 2 == 1, (k + 1) // 2, (ny - k // 2) % ny)

    columns = [((x + h // nc) % nx, (core + h % nc) % nc) for h in range(group)]
    columns = [(x2 * nh * nc + c2, x2 * nc + c2) for x2, c2 in columns]

    def each_peer(act):
        def at(g, first):
            y2 = y + rise(g)
            y2 = jnp.where(y2 >= ny, y2 - ny, y2)
            yh2 = y2 // 2
            act(g, [(yh2 * nc + w, y2 * group + p) for w, p in columns[first:]], y2 - 2 * yh2)

        def step(g, carry):
            at(g, 0)
            return carry

        lax.fori_loop(0, ny - 1, step, 0)
        at(ny - 1, 1)

    def remote(src, dst, send, recv, device):
        return pltpu.make_async_remote_copy(
            src_ref=src, dst_ref=dst, send_sem=send, recv_sem=recv, device_id=device, device_id_type=MESH
        )

    def await_bytes(like, sem):
        pltpu.make_async_copy(like, like, sem).wait()

    def chunk(g):
        y0 = (y + ny - rise(g)) % ny
        return pl.ds(pl.multiple_of(y0 * (8 * group), 8 * group), 8 * group)

    def exchange(source, target, send, recv_of):
        def act(g, devices, yl2):
            for wide2, place2 in devices:
                remote(source(place2), target, send, recv_of(g), (wide2, 2 * z + yl2)).start()

        each_peer(act)

    others = pl.ds(0, 8 * plane - 8)

    loads = [
        pltpu.make_async_copy(src, dst, load_sem.at[i])
        for i, (src, dst) in enumerate((
            (green_in, green), (coulomb_in, vboth.at[yl]), (offsets_in, offsets), (fwd_hi_in, fwd_hi),
            (fwd_lo_in, fwd_lo), (inv_hi_in, inv_hi), (inv_lo_in, inv_lo), (retarded_in, retarded),
        ))
    ]
    for load in loads:
        load.start()

    barrier = pltpu.get_barrier_semaphore()

    def greet(g, devices, yl2):
        for wide2, place2 in devices:
            pl.semaphore_signal(barrier, inc=1, device_id=(wide2, 2 * z + yl2), device_id_type=MESH)

    each_peer(greet)
    for device, there in ((up, has_up), (down, has_down)):
        @pl.when(there)
        def _():
            pl.semaphore_signal(barrier, inc=1, device_id=device, device_id_type=MESH)

    near_receives = jnp.where(yl == 0, has_down, has_up)
    near_sends = jnp.where(yl == 0, has_up, has_down)
    loads[0].wait()

    for i in range(2):
        for pair in range(2):
            for part in range(2):
                for e in range(LOCAL):
                    pack[i, pair, pl.ds(4 * part + e, plane, stride=8), :] = green[
                        pair, part, e, i * plane : (i + 1) * plane, :
                    ]
    pl.semaphore_wait(barrier, plane - 1 + jnp.where(has_up, 1, 0) + jnp.where(has_down, 1, 0))

    own = []
    for i in range(2):
        exchange(
            lambda place2: pack.at[i, :, rows8(place2), :], pairs.at[i, :, yl, rows8(wide), :],
            send_sem.at[0], lambda g: a_sem.at[i],
        )
        own.append(pltpu.make_async_copy(
            pack.at[i, :, rows8(place), :], pairs.at[i, :, yl, rows8(wide), :], local_sem.at[i]
        ))
        own[i].start()
    for load in loads[1:]:
        load.wait()
    for slot in range(2):
        sel[yl, slot] = jnp.where(jnp.full((8, order), offsets[0, slot], jnp.int32) != 0, 1.0, 0.0)
    coulomb_copy = remote(vboth.at[yl], vboth.at[yl], small_send.at[0], small_recv.at[0], partner)
    coulomb_copy.start()
    masks_copy = remote(sel.at[yl], sel.at[yl], small_send.at[1], small_recv.at[1], partner)
    masks_copy.start()

    @pl.when(jnp.logical_not(has_down))
    def _():
        below[...] = jnp.zeros_like(below)

    @pl.when(jnp.logical_not(has_up))
    def _():
        above[...] = jnp.zeros_like(above)

    @pl.when(jnp.logical_not(near_receives))
    def _():
        sigh[...] = jnp.zeros_like(sigh)

    @pl.when(yl == 0)
    def _():
        sig[0] = jnp.zeros(sig.shape[1:], F32)

    tile = min(128, fwd_hi.shape[0])
    for i in range(2):
        own[i].wait()
        await_bytes(pack.at[i, :, others, :], a_sem.at[i])

        def transform(r, carry):
            lesser, greater = pairs[i, 0, r], pairs[i, 1, r]
            conjugate = jnp.where(real_rows(greater.shape), greater, -greater)
            rhs = split(jnp.concatenate([lesser, conjugate], 1))
            for m in range(fwd_hi.shape[0] // tile):
                rows = slice(m * tile, (m + 1) * tile)
                both = dot3((fwd_hi[rows], fwd_lo[rows]), rhs)
                first, second = both[:, :order], both[:, order:]
                lhat[i, r, rows, :] = first
                same, cross = first * second, first * swap(second)
                psend[i, r, rows, :] = jnp.where(real_rows(same.shape), same + swap(same), cross - swap(cross))
            return carry

        lax.fori_loop(0, 2, transform, 0)
        exchange(
            lambda place2: psend.at[i, :, rows8(place2), :], precv.at[i, :, rows8(place), :],
            send_sem.at[1], lambda g: p_sem.at[i, g],
        )
        pltpu.make_async_copy(
            psend.at[i, :, rows8(place), :], precv.at[i, :, rows8(place), :], p_sem.at[i, ny - 1]
        ).start()

    coulomb_copy.wait()
    masks_copy.wait()
    for r in range(2):
        for slot in range(2):
            high, low = split(vboth[r, slot])
            vhi[r, :, slot * order : (slot + 1) * order] = high
            vlo[r, :, slot * order : (slot + 1) * order] = low

    def prepare(e, carry):
        for slot in range(2):
            at = 2 * e + slot
            (rh, rl), (ih, il) = split(retarded[0, e, slot]), split(retarded[1, e, slot])
            for left, right, real, imag in ((left_hi, right_hi, rh, ih), (left_lo, right_lo, rl, il)):
                left[at, :, :order] = real
                left[at, :, order:] = imag
                right[at, :order, :order] = real
                right[at, :order, order:] = -imag
                right[at, order:, :order] = imag
                right[at, order:, order:] = real
        return carry

    lax.fori_loop(0, LOCAL, prepare, 0)

    for i in range(2):
        def forward(g, carry):
            rows = chunk(g)
            await_bytes(precv.at[i, :, rows, :], p_sem.at[i, g])

            @pl.when(has_up)
            def _():
                remote(precv.at[i, 1, rows, :], below.at[i, rows, :], fwd_sem.at[0], up_sem.at[i, g], up).start()

            @pl.when(has_down)
            def _():
                remote(precv.at[i, 0, rows, :], above.at[i, rows, :], fwd_sem.at[1], down_sem.at[i, g], down).start()

            return carry

        lax.fori_loop(0, ny, forward, 0)

    full = 8 * plane
    part_rows = min(256, full)
    for i in range(2):
        def arrive(g, carry):
            rows = chunk(g)

            @pl.when(has_down)
            def _():
                await_bytes(below.at[i, rows, :], up_sem.at[i, g])

            @pl.when(has_up)
            def _():
                await_bytes(above.at[i, rows, :], down_sem.at[i, g])

            return carry

        lax.fori_loop(0, ny, arrive, 0)

        def from_right(m, carry):
            rows = pl.ds(pl.multiple_of(m * part_rows, part_rows), part_rows)
            lower, even, odd, upper = below[i, rows, :], precv[i, 0, rows, :], precv[i, 1, rows, :], above[i, rows, :]
            first = jnp.where(sel[1, 0, 0:1, :] > 0.5, even, odd)
            second = jnp.where(sel[1, 1, 0:1, :] > 0.5, upper, odd)
            for r, slot, value in ((1, 0, first), (1, 1, second), (0, 0, lower), (0, 1, odd)):
                block = slice(slot * order, (slot + 1) * order)
                yy[r, slot, i, rows, :] = dot3(split(value), (vhi[r, :, block], vlo[r, :, block]), True)
            return carry

        lax.fori_loop(0, full // part_rows, from_right, 0)

    own = {}
    for r in (1, 0):
        def from_left(t, carry):
            sides = []
            for part in range(2):
                sides.append(jnp.concatenate(
                    [yy[r, slot, i, pl.ds(4 * part + t, plane, stride=8), :] for slot in range(2) for i in range(2)], 0
                ))
            done = dot3((vhi[r], vlo[r]), split(jnp.concatenate(sides, 1)))
            for part in range(2):
                for i in range(2):
                    zsend[r, i, pl.ds(4 * part + t, plane, stride=8), :] = done[
                        i * plane : (i + 1) * plane, part * order : (part + 1) * order
                    ]
            return carry

        for t in range(LOCAL):
            from_left(t, 0)
        exchange(
            lambda place2: zsend.at[r, :, rows8(place2), :], srecv.at[r, :, rows8(place), :],
            send_sem.at[2], lambda g: s_sem.at[r],
        )
        own[r] = pltpu.make_async_copy(
            zsend.at[r, :, rows8(place), :], srecv.at[r, :, rows8(place), :], local_sem.at[2 + r]
        )
        own[r].start()

    for r in (1, 0):
        own[r].wait()
        await_bytes(zsend.at[r, :, others, :], s_sem.at[r])
        sides = []
        for i in range(2):
            first, second = lhat[i, r], srecv[r, i]
            same, cross = first * second, first * swap(second)
            sides.append(jnp.where(real_rows(same.shape), same - swap(same), cross + swap(cross)))
        rhs = split(jnp.concatenate(sides, 1))
        tile = min(128, inv_hi.shape[0])
        for m in range(inv_hi.shape[0] // tile):
            rows = slice(m * tile, (m + 1) * tile)
            done = dot3((inv_hi[rows], inv_lo[rows]), rhs)
            for i in range(2):
                qsend[r, i, rows, :] = done[:, i * order : (i + 1) * order]

        def send_sigma(g, devices, yl2):
            def send():
                for wide2, place2 in devices:
                    remote(
                        qsend.at[r, :, rows8(wide2), :], sig.at[r, :, rows8(place), :],
                        send_sem.at[3 + r], q_sem.at[r, g], (wide2, 2 * z + yl2),
                    ).start()

            if r == 1:
                send()
            else:
                pl.when(yl2 == 1)(send)

        each_peer(send_sigma)

        def keep():
            pltpu.make_async_copy(
                qsend.at[r, :, rows8(wide), :], sig.at[r, :, rows8(place), :], q_sem.at[r, ny - 1]
            ).start()

        if r == 1:
            keep()
        else:
            pl.when(yl == 1)(keep)

    for r, parity, device in ((1, 0, up), (0, 1, down)):
        def spread(g, carry):
            rows = chunk(g)
            await_bytes(sig.at[r, :, rows, :], q_sem.at[r, g])

            @pl.when(jnp.logical_and(near_sends, yl == parity))
            def _():
                remote(sig.at[r, :, rows, :], sigh.at[:, rows, :], fwd_sem.at[2], h_sem.at[g], device).start()

            return carry

        if r == 1:
            lax.fori_loop(0, ny, spread, 0)
        else:
            @pl.when(yl == 1)
            def _():
                lax.fori_loop(0, ny, spread, 0)

    def term(at, real, imag):
        left = dot3(
            (left_hi[at], left_lo[at]),
            split(jnp.concatenate([jnp.concatenate([real, imag], 1), jnp.concatenate([-imag, real], 1)], 0)),
        )
        return dot3(split(left), (right_hi[at], right_lo[at]), True)

    def block(ref, e, part, *lead):
        return jnp.concatenate(
            [ref[(*lead, i, pl.ds(4 * part + e, plane, stride=8), slice(None))] for i in range(2)], 0
        )

    odd_cell = jnp.full((8, order), yl, jnp.int32) == 1
    take_near = jnp.logical_and(odd_cell, sel[yl, 0] > 0.5)[0:1]
    take_far = jnp.logical_or(jnp.logical_not(odd_cell), sel[yl, 1] > 0.5)[0:1]
    for e in range(LOCAL):
        real, imag = (jnp.where(take_near, block(sig, e, part, 0), block(sig, e, part, 1)) for part in range(2))
        done = term(2 * e + 1 - yl, real, imag)
        out[0, e] = done[:, :order]
        out[1, e] = done[:, order:]

    def arrive_far(g, carry):
        await_bytes(sigh.at[:, chunk(g), :], h_sem.at[g])
        return carry

    @pl.when(near_receives)
    def _():
        lax.fori_loop(0, ny, arrive_far, 0)

    for e in range(LOCAL):
        real, imag = (jnp.where(take_far, block(sigh, e, part), block(sig, e, part, 1)) for part in range(2))
        done = term(2 * e + yl, real, imag)
        out[0, e] += done[:, :order]
        out[1, e] += done[:, order:]

    for phase, ref in enumerate((pack, psend, zsend)):
        await_bytes(ref.at[:, :, others, :], send_sem.at[phase])
    await_bytes(sig.at[1, :, others, :], send_sem.at[4])

    @pl.when(yl == 0)
    def _():
        await_bytes(sig.at[0, :, pl.ds(0, 4 * plane), :], send_sem.at[3])

    @pl.when(yl == 1)
    def _():
        await_bytes(sig.at[0, :, pl.ds(0, 4 * plane - 8), :], send_sem.at[3])

    @pl.when(has_up)
    def _():
        await_bytes(below, fwd_sem.at[0])

    @pl.when(has_down)
    def _():
        await_bytes(above, fwd_sem.at[1])

    @pl.when(near_sends)
    def _():
        await_bytes(sigh, fwd_sem.at[2])


def body(green_pair, coulomb, green_retarded, offsets):
    nx, nh, nc = WIDE_PARTS
    ny, plane = 2 * nh, 2 * nx * nh * nc
    order, local = green_pair.shape[-1], green_pair.shape[2]
    energies = local * nx * nh * nc
    full = 8 * plane
    consts = [jnp.asarray(value) for value in tables(energies)]
    hbm = pl.BlockSpec(memory_space=pltpu.HBM)
    arguments = (green_pair[:, :, :, 0], coulomb[0], offsets, green_retarded[:, :, 0], *consts)
    dma = pltpu.SemaphoreType.DMA
    dressed = pl.pallas_call(
        kernel,
        out_shape=jax.ShapeDtypeStruct((2, local, order, order), F32),
        in_specs=[hbm] * len(arguments),
        out_specs=pl.BlockSpec(memory_space=pltpu.VMEM),
        scratch_shapes=[
            pltpu.VMEM(arguments[0].shape, F32),
            pltpu.VMEM(arguments[3].shape, F32),
            *(pltpu.VMEM(value.shape, BF16) for value in consts),
            pltpu.SMEM((1, 2), jnp.int32),
            pltpu.VMEM((2, 2, full, order), F32),
            pltpu.VMEM((2, 2, 2, full // 2, order), F32),
            pltpu.VMEM((2, 2, full, order), F32),
            pltpu.VMEM((2, 2, full, order), F32),
            pltpu.VMEM((2, 2, full, order), F32),
            pltpu.VMEM((2, full, order), F32),
            pltpu.VMEM((2, full, order), F32),
            pltpu.VMEM((2, 2, order, order), F32),
            pltpu.VMEM((2, order, 2 * order), BF16),
            pltpu.VMEM((2, order, 2 * order), BF16),
            pltpu.VMEM((2, 2, 8, order), F32),
            pltpu.VMEM((2, 2, 2, full, order), F32),
            pltpu.VMEM((2, 2, full, order), F32),
            pltpu.VMEM((2, 2, full, order), F32),
            pltpu.VMEM((2, 2, full // 2, order), F32),
            pltpu.VMEM((2, 2, full, order), F32),
            pltpu.VMEM((2, full, order), F32),
            *[pltpu.VMEM((2 * local, order, 2 * order), BF16)] * 2,
            *[pltpu.VMEM((2 * local, 2 * order, 2 * order), BF16)] * 2,
            dma((8,)), dma((4,)), dma((2,)), dma((2,)), dma((5,)), dma((2,)), dma((2, ny)), dma((2, ny)), dma((2, ny)),
            dma((2,)), dma((2, ny)), dma((ny,)), dma((3,)),
        ],
        compiler_params=pltpu.CompilerParams(
            collective_id=0, has_side_effects=True, vmem_limit_bytes=60 * 1024 * 1024
        ),
    )(*arguments)
    return dressed[:, :, None]


def solution(mesh):
    placed = (
        P(None, None, "wide", "cell", None, None),
        P("cell", None, None, None),
        P(None, "wide", "cell", None, None, None),
        P("cell", None),
    )
    return jax.shard_map(
        body,
        mesh=mesh,
        in_specs=placed,
        out_specs=P(None, "wide", "cell", None, None),
        check_vma=False,
    )
```

time: 147 us -> 131 us (0.89)
  Pallas kernels: 137 us -> 129 us
  local copies, waits for them, and re-layouts: 8.6 us -> 1.87 us
    pallas_call x1, Pallas kernels: 137 us -> 129 us  [body(): pl.pallas_call(kernel, out_shape=jax.ShapeDtypeStruct((2, local, order, o...]
    unnamed x17 -> x1, local copies, waits for them, and re-layouts: 8.6 us -> 1.87 us
where the time goes in v1:
time: 131 us; the launch traced here: 130 us
  Pallas kernels  129 us (98%)
  local copies, waits for them, and re-layouts  1.87 us (1%)
    pallas_call x1, Pallas kernels, body(): pl.pallas_call(kernel, out_shape=jax.ShapeDtypeStruct((2, local, order, o...  129 us

profile of v1, /device:TPU:56, one launch (start us, length us, event | category | flops | bytes accessed | tf_op | source)
XLA Modules:
  0.0 130.4 jit_solution(14223307393118050823)
XLA Ops:
  0.0 128.5 %shard_map.82 = f32[2,4,128,128]{3,2,1,0:T(8,128)} custom-call(f32[2,2,4,128,128]{4,3,2,1,0:T(8,128)} %bitcast.7, f32[2,128,128]{2,1,0:T(8,128)} %bitcast.9, s32[1,2]{1,0:T(1,128)} %offsets_in.1, f32[2,4,2,128,128]{4,3,2,1,0:T(8,128)} %bitcast.8, bf16[512,256]{1,0:T(8,128)(2,1)} %constant.8.clone.fwd_hi_in, bf16[512,256]{1,0:T(8,128)(2,1)} %constant.9.clone.fwd_lo_in, ...), custom_call_target="tpu_custom_call" | custom-call | tf_op jit(solution)/shard_map/pallas_call | solution.py:449
  128.5 1.9 %copy.11 = f32[2,4,1,128,128]{4,3,2,1,0:T(8,128)} copy(f32[2,4,1,128,128]{4,3,2,1,0:T(8,128)} %bitcast.6) | data formatting | bytes 1048576

commit v2 on v1

--- a/solution.py
+++ b/solution.py
@@ -59,9 +59,9 @@
 def kernel(
     green_in, coulomb_in, offsets_in, retarded_in, fwd_hi_in, fwd_lo_in, inv_hi_in, inv_lo_in, out,
     green, retarded, fwd_hi, fwd_lo, inv_hi, inv_lo, offsets,
-    pack, pairs, lhat, psend, precv, below, above, vboth, vhi, vlo, sel, yy, zsend, srecv, qsend, sig, sigh,
+    pack, pairs, lhat, psend, precv, below, above, vboth, vhi, vlo, sel, yy, zsend, srecv, qsend, qhalo, xsend, sig,
     left_hi, left_lo, right_hi, right_lo,
-    load_sem, local_sem, small_send, small_recv, send_sem, a_sem, p_sem, up_sem, down_sem, s_sem, q_sem, h_sem, fwd_sem,
+    load_sem, local_sem, small_send, small_recv, send_sem, a_sem, p_sem, up_sem, down_sem, s_sem, q_sem, h_sem, x_sem, halo_sem, fwd_sem,
 ):
     wide, cell = lax.axis_index("wide"), lax.axis_index("cell")
     cells = lax.axis_size("cell")
@@ -145,8 +145,7 @@
         def _():
             pl.semaphore_signal(barrier, inc=1, device_id=device, device_id_type=MESH)
 
-    near_receives = jnp.where(yl == 0, has_down, has_up)
-    near_sends = jnp.where(yl == 0, has_up, has_down)
+    even_sends, even_receives = jnp.logical_and(yl == 0, has_up), jnp.logical_and(yl == 0, has_down)
     loads[0].wait()
 
     for i in range(2):
@@ -184,12 +183,9 @@
     @pl.when(jnp.logical_not(has_up))
     def _():
         above[...] = jnp.zeros_like(above)
-
-    @pl.when(jnp.logical_not(near_receives))
-    def _():
-        sigh[...] = jnp.zeros_like(sigh)
-
-    @pl.when(yl == 0)
+        qhalo[...] = jnp.zeros_like(qhalo)
+
+    @pl.when(jnp.logical_and(yl == 0, jnp.logical_not(has_down)))
     def _():
         sig[0] = jnp.zeros(sig.shape[1:], F32)
 
@@ -317,7 +313,7 @@
         )
         own[r].start()
 
-    for r in (1, 0):
+    def self_energy(r):
         own[r].wait()
         await_bytes(zsend.at[r, :, others, :], s_sem.at[r])
         sides = []
@@ -333,48 +329,55 @@
             for i in range(2):
                 qsend[r, i, rows, :] = done[:, i * order : (i + 1) * order]
 
-        def send_sigma(g, devices, yl2):
-            def send():
+    def send_sigma(source, slot, parity, send, recv_of):
+        def act(g, devices, yl2):
+            @pl.when(yl2 == parity)
+            def _():
                 for wide2, place2 in devices:
                     remote(
-                        qsend.at[r, :, rows8(wide2), :], sig.at[r, :, rows8(place), :],
-                        send_sem.at[3 + r], q_sem.at[r, g], (wide2, 2 * z + yl2),
+                        source.at[:, rows8(wide2), :], sig.at[slot, :, rows8(place), :],
+                        send, recv_of(g), (wide2, 2 * z + parity),
                     ).start()
 
-            if r == 1:
-                send()
-            else:
-                pl.when(yl2 == 1)(send)
-
-        each_peer(send_sigma)
-
-        def keep():
+        each_peer(act)
+
+        @pl.when(yl == parity)
+        def _():
             pltpu.make_async_copy(
-                qsend.at[r, :, rows8(wide), :], sig.at[r, :, rows8(place), :], q_sem.at[r, ny - 1]
+                source.at[:, rows8(wide), :], sig.at[slot, :, rows8(place), :], recv_of(ny - 1)
             ).start()
 
-        if r == 1:
-            keep()
-        else:
-            pl.when(yl == 1)(keep)
-
-    for r, parity, device in ((1, 0, up), (0, 1, down)):
-        def spread(g, carry):
-            rows = chunk(g)
-            await_bytes(sig.at[r, :, rows, :], q_sem.at[r, g])
-
-            @pl.when(jnp.logical_and(near_sends, yl == parity))
-            def _():
-                remote(sig.at[r, :, rows, :], sigh.at[:, rows, :], fwd_sem.at[2], h_sem.at[g], device).start()
-
-            return carry
-
-        if r == 1:
-            lax.fori_loop(0, ny, spread, 0)
-        else:
-            @pl.when(yl == 1)
-            def _():
-                lax.fori_loop(0, ny, spread, 0)
+    self_energy(1)
+    send_sigma(qsend.at[1], 1, 0, send_sem.at[3], lambda g: q_sem.at[g])
+    self_energy(0)
+
+    @pl.when(has_down)
+    def _():
+        remote(qsend.at[0], qhalo, fwd_sem.at[3], halo_sem, down).start()
+
+    xsend[0] = jnp.where(sel[1, 0, 0:1, :] > 0.5, qsend[0], qsend[1])
+    send_sigma(xsend.at[0], 0, 1, send_sem.at[4], lambda g: x_sem.at[0])
+
+    def spread(g, carry):
+        rows = chunk(g)
+        await_bytes(sig.at[1, :, rows, :], q_sem.at[g])
+
+        @pl.when(has_up)
+        def _():
+            remote(sig.at[1, :, rows, :], sig.at[0, :, rows, :], fwd_sem.at[2], h_sem.at[g], up).start()
+
+        return carry
+
+    @pl.when(yl == 0)
+    def _():
+        lax.fori_loop(0, ny, spread, 0)
+
+    @pl.when(has_up)
+    def _():
+        await_bytes(qhalo, halo_sem)
+
+    xsend[1] = jnp.where(sel[1, 1, 0:1, :] > 0.5, qhalo[...], qsend[1])
+    send_sigma(xsend.at[1], 1, 1, send_sem.at[5], lambda g: x_sem.at[1])
 
     def term(at, real, imag):
         left = dot3(
@@ -383,45 +386,47 @@
         )
         return dot3(split(left), (right_hi[at], right_lo[at]), True)
 
-    def block(ref, e, part, *lead):
-        return jnp.concatenate(
-            [ref[(*lead, i, pl.ds(4 * part + e, plane, stride=8), slice(None))] for i in range(2)], 0
-        )
-
-    odd_cell = jnp.full((8, order), yl, jnp.int32) == 1
-    take_near = jnp.logical_and(odd_cell, sel[yl, 0] > 0.5)[0:1]
-    take_far = jnp.logical_or(jnp.logical_not(odd_cell), sel[yl, 1] > 0.5)[0:1]
+    def dress(e, slot):
+        real, imag = (
+            jnp.concatenate([sig[slot, i, pl.ds(4 * part + e, plane, stride=8), :] for i in range(2)], 0)
+            for part in range(2)
+        )
+        return term(2 * e + slot, real, imag)
+
+    @pl.when(yl == 1)
+    def _():
+        await_bytes(sig.at[0], x_sem.at[0])
+
     for e in range(LOCAL):
-        real, imag = (jnp.where(take_near, block(sig, e, part, 0), block(sig, e, part, 1)) for part in range(2))
-        done = term(2 * e + 1 - yl, real, imag)
+        done = dress(e, 1 - yl)
         out[0, e] = done[:, :order]
         out[1, e] = done[:, order:]
 
+    @pl.when(yl == 1)
+    def _():
+        await_bytes(sig.at[1], x_sem.at[1])
+
     def arrive_far(g, carry):
-        await_bytes(sigh.at[:, chunk(g), :], h_sem.at[g])
+        await_bytes(sig.at[0, :, chunk(g), :], h_sem.at[g])
         return carry
 
-    @pl.when(near_receives)
+    @pl.when(even_receives)
     def _():
         lax.fori_loop(0, ny, arrive_far, 0)
 
     for e in range(LOCAL):
-        real, imag = (jnp.where(take_far, block(sigh, e, part), block(sig, e, part, 1)) for part in range(2))
-        done = term(2 * e + yl, real, imag)
+        done = dress(e, yl)
         out[0, e] += done[:, :order]
         out[1, e] += done[:, order:]
 
     for phase, ref in enumerate((pack, psend, zsend)):
         await_bytes(ref.at[:, :, others, :], send_sem.at[phase])
-    await_bytes(sig.at[1, :, others, :], send_sem.at[4])
-
-    @pl.when(yl == 0)
-    def _():
-        await_bytes(sig.at[0, :, pl.ds(0, 4 * plane), :], send_sem.at[3])
-
-    @pl.when(yl == 1)
-    def _():
-        await_bytes(sig.at[0, :, pl.ds(0, 4 * plane - 8), :], send_sem.at[3])
+    for parity in range(2):
+        @pl.when(yl == parity)
+        def _():
+            for phase in (3, 4, 5):
+                fewer = 8 if (phase == 3) == (parity == 0) else 0
+                await_bytes(sig.at[0, :, pl.ds(0, 4 * plane - fewer), :], send_sem.at[phase])
 
     @pl.when(has_up)
     def _():
@@ -430,10 +435,11 @@
     @pl.when(has_down)
     def _():
         await_bytes(above, fwd_sem.at[1])
-
-    @pl.when(near_sends)
-    def _():
-        await_bytes(sigh, fwd_sem.at[2])
+        await_bytes(qhalo, fwd_sem.at[3])
+
+    @pl.when(even_sends)
+    def _():
+        await_bytes(sig.at[0], fwd_sem.at[2])
 
 
 def body(green_pair, coulomb, green_retarded, offsets):
@@ -471,12 +477,13 @@
             pltpu.VMEM((2, 2, full, order), F32),
             pltpu.VMEM((2, 2, full, order), F32),
             pltpu.VMEM((2, 2, full // 2, order), F32),
-            pltpu.VMEM((2, 2, full, order), F32),
-            pltpu.VMEM((2, full, order), F32),
+            pltpu.VMEM((2, full // 2, order), F32),
+            pltpu.VMEM((2, 2, full // 2, order), F32),
+            pltpu.VMEM((2, 2, full, order), F32),
             *[pltpu.VMEM((2 * local, order, 2 * order), BF16)] * 2,
             *[pltpu.VMEM((2 * local, 2 * order, 2 * order), BF16)] * 2,
-            dma((8,)), dma((4,)), dma((2,)), dma((2,)), dma((5,)), dma((2,)), dma((2, ny)), dma((2, ny)), dma((2, ny)),
-            dma((2,)), dma((2, ny)), dma((ny,)), dma((3,)),
+            dma((8,)), dma((4,)), dma((2,)), dma((2,)), dma((6,)), dma((2,)), dma((2, ny)), dma((2, ny)), dma((2, ny)),
+            dma((2,)), dma((ny,)), dma((ny,)), dma((2,)), dma, dma((4,)),
         ],
         compiler_params=pltpu.CompilerParams(
             collective_id=0, has_side_effects=True, vmem_limit_bytes=60 * 1024 * 1024

time: 131 us -> 121 us (0.924); the launches traced: 130 us -> 119 us
  Pallas kernels: 129 us -> 117 us
    pallas_call x1, Pallas kernels: 129 us -> 117 us  [body(): pl.pallas_call(kernel, out_shape=jax.ShapeDtypeStruct((2, local, order, o...]
where the time goes in v2:
time: 121 us; the launch traced here: 119 us
  Pallas kernels  117 us (97%)
  local copies, waits for them, and re-layouts  1.87 us (2%)
    pallas_call x1, Pallas kernels, body(): pl.pallas_call(kernel, out_shape=jax.ShapeDtypeStruct((2, local, order, o...  117 us

profile of v2, /device:TPU:56, one launch (start us, length us, event | category | flops | bytes accessed | tf_op | source)
XLA Modules:
  0.0 118.7 jit_solution(11638190134488356903)
XLA Ops:
  0.0 116.8 %shard_map.82 = f32[2,4,128,128]{3,2,1,0:T(8,128)} custom-call(f32[2,2,4,128,128]{4,3,2,1,0:T(8,128)} %bitcast.7, f32[2,128,128]{2,1,0:T(8,128)} %bitcast.9, s32[1,2]{1,0:T(1,128)} %offsets_in.1, f32[2,4,2,128,128]{4,3,2,1,0:T(8,128)} %bitcast.8, bf16[512,256]{1,0:T(8,128)(2,1)} %constant.8.clone.fwd_hi_in, bf16[512,256]{1,0:T(8,128)(2,1)} %constant.9.clone.fwd_lo_in, ...), custom_call_target="tpu_custom_call" | custom-call | tf_op jit(solution)/shard_map/pallas_call | solution.py:455
  116.8 1.9 %copy.11 = f32[2,4,1,128,128]{4,3,2,1,0:T(8,128)} copy(f32[2,4,1,128,128]{4,3,2,1,0:T(8,128)} %bitcast.6) | data formatting | bytes 1048576

commit v3 on v2

--- a/solution.py
+++ b/solution.py
@@ -148,17 +148,21 @@
     even_sends, even_receives = jnp.logical_and(yl == 0, has_up), jnp.logical_and(yl == 0, has_down)
     loads[0].wait()
 
-    for i in range(2):
+    def pack_half(i):
         for pair in range(2):
             for part in range(2):
                 for e in range(LOCAL):
                     pack[i, pair, pl.ds(4 * part + e, plane, stride=8), :] = green[
                         pair, part, e, i * plane : (i + 1) * plane, :
                     ]
+
+    pack_half(0)
     pl.semaphore_wait(barrier, plane - 1 + jnp.where(has_up, 1, 0) + jnp.where(has_down, 1, 0))
 
     own = []
     for i in range(2):
+        if i == 1:
+            pack_half(1)
         exchange(
             lambda place2: pack.at[i, :, rows8(place2), :], pairs.at[i, :, yl, rows8(wide), :],
             send_sem.at[0], lambda g: a_sem.at[i],
@@ -258,36 +262,32 @@
 
     full = 8 * plane
     part_rows = min(256, full)
-    for i in range(2):
-        def arrive(g, carry):
-            rows = chunk(g)
-
-            @pl.when(has_down)
+    own = {}
+    for r, halo, there, sems in ((1, above, has_up, down_sem), (0, below, has_down, up_sem)):
+        for i in range(2):
+            @pl.when(there)
             def _():
-                await_bytes(below.at[i, rows, :], up_sem.at[i, g])
-
-            @pl.when(has_up)
-            def _():
-                await_bytes(above.at[i, rows, :], down_sem.at[i, g])
-
-            return carry
-
-        lax.fori_loop(0, ny, arrive, 0)
-
-        def from_right(m, carry):
-            rows = pl.ds(pl.multiple_of(m * part_rows, part_rows), part_rows)
-            lower, even, odd, upper = below[i, rows, :], precv[i, 0, rows, :], precv[i, 1, rows, :], above[i, rows, :]
-            first = jnp.where(sel[1, 0, 0:1, :] > 0.5, even, odd)
-            second = jnp.where(sel[1, 1, 0:1, :] > 0.5, upper, odd)
-            for r, slot, value in ((1, 0, first), (1, 1, second), (0, 0, lower), (0, 1, odd)):
-                block = slice(slot * order, (slot + 1) * order)
-                yy[r, slot, i, rows, :] = dot3(split(value), (vhi[r, :, block], vlo[r, :, block]), True)
-            return carry
-
-        lax.fori_loop(0, full // part_rows, from_right, 0)
-
-    own = {}
-    for r in (1, 0):
+                def arrive(g, carry):
+                    await_bytes(halo.at[i, chunk(g), :], sems.at[i, g])
+                    return carry
+
+                lax.fori_loop(0, ny, arrive, 0)
+
+            def from_right(m, carry):
+                rows = pl.ds(pl.multiple_of(m * part_rows, part_rows), part_rows)
+                other, odd = halo[i, rows, :], precv[i, 1, rows, :]
+                if r == 1:
+                    first = jnp.where(sel[1, 0, 0:1, :] > 0.5, precv[i, 0, rows, :], odd)
+                    second = jnp.where(sel[1, 1, 0:1, :] > 0.5, other, odd)
+                else:
+                    first, second = other, odd
+                for slot, value in ((0, first), (1, second)):
+                    block = slice(slot * order, (slot + 1) * order)
+                    yy[r, slot, i, rows, :] = dot3(split(value), (vhi[r, :, block], vlo[r, :, block]), True)
+                return carry
+
+            lax.fori_loop(0, full // part_rows, from_right, 0)
+
         def from_left(t, carry):
             sides = []
             for part in range(2):

time: 121 us -> 120 us (level)
  no operation moved by 1% of the time
where the time goes in v3:
time: 120 us; the launch traced here: 118 us
  Pallas kernels  116 us (97%)
  local copies, waits for them, and re-layouts  1.87 us (2%)
    pallas_call x1, Pallas kernels, body(): pl.pallas_call(kernel, out_shape=jax.ShapeDtypeStruct((2, local, order, o...  116 us

profile of v3, /device:TPU:56, one launch (start us, length us, event | category | flops | bytes accessed | tf_op | source)
XLA Modules:
  0.0 117.7 jit_solution(7048402546405998353)
XLA Ops:
  0.0 115.8 %shard_map.82 = f32[2,4,128,128]{3,2,1,0:T(8,128)} custom-call(f32[2,2,4,128,128]{4,3,2,1,0:T(8,128)} %bitcast.7, f32[2,128,128]{2,1,0:T(8,128)} %bitcast.9, s32[1,2]{1,0:T(1,128)} %offsets_in.1, f32[2,4,2,128,128]{4,3,2,1,0:T(8,128)} %bitcast.8, bf16[512,256]{1,0:T(8,128)(2,1)} %constant.8.clone.fwd_hi_in, bf16[512,256]{1,0:T(8,128)(2,1)} %constant.9.clone.fwd_lo_in, ...), custom_call_target="tpu_custom_call" | custom-call | tf_op jit(solution)/shard_map/pallas_call | solution.py:455
  115.8 1.9 %copy.11 = f32[2,4,1,128,128]{4,3,2,1,0:T(8,128)} copy(f32[2,4,1,128,128]{4,3,2,1,0:T(8,128)} %bitcast.6) | data formatting | bytes 1048576
